TPU v7x, 256 devices: a whole 4x4x8 slice. The times are simulated.
256 devices in a mesh: param: 64 (over z, x, core), tok: 2 (over y_lo), probe: 2 (over y_hi).
Axes of the slice: x: 4, y: 4 (y_hi: 2, y_lo: 2; y = y_hi * 2 + y_lo), z: 8, core: 2. Of those that a mesh axis runs over, the one named last changes fastest.
Arguments:
- tokens_x: bfloat16 [1024, 8192], P('tok'), may hold values from -6 to 6
- cotangent: bfloat16 [2, 1024, 14336], P('probe', 'tok', 'param'), may hold values from -6 to 6
- signs: int32 [134217728], P(('param', 'tok')), may hold values from -1 to 1, as said below
- samples: int32 [16384], replicated, may hold values from 0 to 134217727
Outputs:
- sketch: float32 [2, 16384], P(None, 'probe')
- basis: float32 [2, 16384], P(None, 'probe')
Inputs may be any that keep to these rules, and one draw needn't show every extreme that they name: `signs`: every entry is +1 or -1.
All inputs are finite; a program needn't handle non-finite values.
Results may differ from a plain program's by a relative error of at most 0.0003.
Values sent between devices are 32-bit elements; how exact they have to be, the bound alone decides.
A program may use at most 128 MiB of HBM per device.

v0:
```python
import jax
import jax.numpy as jnp
from jax import lax
from jax.sharding import PartitionSpec as P


def bit_parity(value, bits):
    total = jnp.zeros_like(value)
    for shift_bit in range(bits):
        total = total + (value >> shift_bit & 1)
    return total & 1


def hadamard_table(width):
    index = jnp.arange(width, dtype=jnp.int32)
    parity = bit_parity(index[:, None] & index[None, :], width.bit_length())
    return (1 - 2 * parity).astype(jnp.float32)


def hadamard(vector):
    length = vector.shape[0]
    total_bits = length.bit_length() - 1
    done = 0
    while done < total_bits:
        step_bits = min(7, total_bits - done)
        width = 2**step_bits
        table = hadamard_table(width)
        if done == 0:
            vector = jnp.dot(vector.reshape(-1, width), table, precision=lax.Precision.HIGHEST)
        else:
            shaped = vector.reshape(length // 2 ** (done + step_bits), width, 2**done)
            vector = jnp.einsum("fg,agb->afb", table, shaped, precision=lax.Precision.HIGHEST)
        vector = vector.reshape(length)
        done = done + step_bits
    return vector


def on_device(tokens_x, cotangent, signs, samples):
    local_len = signs.shape[0]
    width_rows = tokens_x.shape[1]
    tok_count = lax.axis_size("tok")
    group_size = lax.axis_size(("param", "tok"))
    pad_width = local_len * tok_count // width_rows
    col_count = cotangent.shape[2]
    local_cot = cotangent[0]
    scale = float(tokens_x.shape[0] * tok_count * local_len * group_size) ** (-0.5)
    product = jnp.einsum("tr,tc->rc", tokens_x, local_cot, preferred_element_type=jnp.float32)
    summed = lax.psum_scatter(
        jnp.pad(product, ((0, 0), (0, pad_width - col_count))),
        "tok",
        scatter_dimension=0,
        tiled=True,
    )
    signed = summed.reshape(local_len) * signs.astype(jnp.float32)
    mixed = hadamard(signed)
    my_index = lax.axis_index(("param", "tok"))
    high_part = samples // local_len
    low_part = samples % local_len
    block_len = local_len // group_size
    pieces = lax.all_to_all(
        mixed.reshape(group_size, block_len),
        ("param", "tok"),
        split_axis=0,
        concat_axis=0,
        tiled=True,
    )
    finished = jnp.dot(hadamard_table(group_size), pieces, precision=lax.Precision.HIGHEST)
    position = high_part * block_len + low_part % block_len
    owned = low_part // block_len == my_index
    values = jnp.where(owned, jnp.take(finished.reshape(-1), position), 0.0)
    sketch_row = lax.psum(values, ("param", "tok"))
    sketch_row = sketch_row * scale
    sketch = lax.all_to_all(sketch_row[None, :], "probe", split_axis=1, concat_axis=0, tiled=True)
    total_rows = float(sketch.shape[1] * lax.axis_size("probe"))
    first = sketch[0]
    second_raw = sketch[1]
    mean_first = lax.psum(jnp.sum(first * first) / total_rows, "probe") + 1e-06
    unit = first * lax.rsqrt(mean_first)
    proj = lax.psum(jnp.sum(unit * second_raw) / total_rows, "probe")
    rest = second_raw - proj * unit
    mean_rest = lax.psum(jnp.sum(rest * rest) / total_rows, "probe") + 1e-06
    second = rest * lax.rsqrt(mean_rest)
    basis = jnp.stack([unit, second])
    return (sketch, basis)


def solution(mesh):
    in_specs = (P("tok", None), P("probe", "tok", "param"), P(("param", "tok")), P())
    out_specs = (P(None, "probe"), P(None, "probe"))
    return jax.shard_map(
        on_device, mesh=mesh, in_specs=in_specs, out_specs=out_specs, check_vma=False
    )
```

profile of v0, /device:TPU:1, one launch (start us, length us, event | category | flops | bytes accessed | tf_op | source)
XLA Modules:
  0.0 1446.0 jit_solution(4617305056931093167)
XLA Ops:
  7.2 0.0 copy-start
  7.2 0.0 reduce-scatter.2.cloned.1.call-start
  7.2 0.9 copy-done
  8.1 5.5 fusion.8
  13.6 4.1 pad.4
  17.7 0.0 reduce-scatter.2.cloned.1.call-update
  17.7 108.3 %reduce-scatter.2.cloned.1.call-done = f32[4096,256]{0,1:T(8,128)} async-done(((f32[8192,256]{0,1:T(8,128)}), f32[4096,256]{0,1:T(8,128)}) %reduce-scatter.2.cloned.1.call-update) | async-done | bytes 4194320 | tf_op jit(solution)/shard_map/reduce_scatter | solution.py:48
  126.0 5.6 copy.8
  131.6 0.0 copy-start.2
  131.6 4.5 copy.15
  136.1 0.0 copy-done.2
  136.1 0.4 convert_multiply_fusion
  136.5 4.2 fusion.14
  140.8 5.0 convolution_bitcast_fusion.1
  145.8 5.6 copy.10
  151.4 10.4 convolution_bitcast_fusion
  161.8 7.7 all_to_all.29
  169.4 0.0 copy-start.3
  169.4 12.1 all-to-all-start
  181.5 0.0 all-reduce.3.cloned.1.call-start
  181.5 0.0 copy-done.3
  181.5 0.1 broadcast_clamp_fusion
  181.7 96.2 %all-to-all-done = f32[128,1,8192]{2,1,0:T(1,128)} async-done(((f32[128,1,8192]{2,1,0:T(1,128)}), f32[128,1,8192]{2,1,0:T(1,128)}, u32[]{:S(2)}, u32[]{:S(2)}) %all-to-all-start) | async-done | bytes 4194336 | tf_op jit(solution)/shard_map/all_to_all | solution.py:60
  277.8 8.3 fusion.5
  286.2 2.7 copy.17
  288.8 0.0 copy-start.1
  288.8 192.1 %gather_fusion = f32[16384]{0:T(1024)S(1)} fusion(f32[1048576]{0:T(1024)} %bitcast.39, s32[16384]{0:T(1024)S(1)} %broadcast_clamp_fusion), kind=kCustom, calls=%fused_computation | custom fusion | bytes 196608 | tf_op jit(solution)/shard_map/jit(_take)/gather | solution.py:70
  480.9 0.8 select_select_fusion
  481.7 0.0 all-reduce.3.cloned.1.call-update
  481.7 923.3 %all-reduce.3.cloned.1.call-done = f32[16384]{0:T(1024)} async-done(((f32[16384]{0:T(1024)}), f32[16384]{0:T(1024)}) %all-reduce.3.cloned.1.call-update) | async-done | bytes 65552 | tf_op jit(solution)/shard_map/psum | solution.py:71
  1405.0 0.8 broadcast_multiply_fusion
  1405.8 8.0 all_to_all.32
  1413.8 0.7 multiply_reduce_fusion.2
  1415.1 5.8 psum.29
  1421.6 0.6 multiply_reduce_fusion.1
  1422.9 5.8 psum.30
  1428.7 1.3 multiply_reduce_fusion
  1430.6 5.8 psum.31
  1437.1 0.7 subtract_multiply_fusion
  1437.8 0.7 pad_maximum_fusion
  1438.5 0.7 copy.29
  1439.2 0.0 copy-done.1
  (1 shorter events, 0.0 us)
Async XLA Ops:
  7.2 0.9 copy-start
  7.2 118.8 %reduce-scatter.2.cloned.1.call-start = ((), (), s32[]{:S(2)}) async-start(), calls=%async_computation.3 | async-start | bytes 12582912 | tf_op jit(solution)/shard_map/reduce_scatter | solution.py:48
  131.6 4.5 copy-start.2
  169.4 12.1 copy-start.3
  169.4 108.4 %all-to-all-start = ((f32[128,1,8192]{2,1,0:T(1,128)}), f32[128,1,8192]{2,1,0:T(1,128)}, u32[]{:S(2)}, u32[]{:S(2)}) async-start(f32[128,1,8192]{2,1,0:T(1,128)} %all_to_all.29), calls=%async_computation.1 | async-start | bytes 8388608 | tf_op jit(solution)/shard_map/all_to_all | solution.py:60
  181.5 1223.5 %all-reduce.3.cloned.1.call-start = ((), (), s32[]{:S(2)}) async-start(), calls=%async_computation.4 | async-start | bytes 131072 | tf_op jit(solution)/shard_map/psum | solution.py:71
  288.8 1150.3 %copy-start.1 = (bf16[1,512,224]{1,2,0:T(8,128)(2,1)S(1)}, bf16[1,512,224]{1,2,0:T(8,128)(2,1)}, u32[]{:S(2)}) copy-start(bf16[1,512,224]{1,2,0:T(8,128)(2,1)} %param.5) | copy-start | bytes 688132
Sparse Core Ops, SparseCore 0:
  17.9 108.1 reduce-scatter.1
  481.8 923.1 all-reduce.2
where the time goes:
time: 1460 us; the launch traced here: 1450 us
  waiting for transfers between devices  1130 us (77%)
  local copies, waits for them, and re-layouts  224 us (15%)
  matrix products  33.4 us (2%)
  blocking collectives  25.4 us (2%)
  between operations  17.5 us (1%)
    psum x1, waiting for transfers between devices, on_device(): sketch_row = lax.psum(values, ('param', 'tok'))  923 us
    gather x1, local copies, waits for them, and re-layouts, on_device(): values = jnp.where(owned, jnp.take(finished.reshape(-1), position), 0.0)  192 us
    reduce_scatter x1, waiting for transfers between devices, on_device(): lax.psum_scatter(jnp.pad(product, ((0, 0), (0, pad_width - col_count))),...  108 us
    all_to_all x1, waiting for transfers between devices, on_device(): lax.all_to_all(mixed.reshape(group_size, block_len), ('param', 'tok'), sp...  96.2 us
  transfers between devices with their start and end apart: 3, of which 3 were waited for; matrix products, arithmetic and copies ran while one was open for 0% of the time, Pallas kernels for 0%

commit v1 on v0

v1 whole, which is shorter than its diff:
```python
import functools

import jax
import jax.numpy as jnp
from jax import lax
from jax.experimental import pallas as pl
from jax.experimental.pallas import tpu as pltpu
from jax.sharding import PartitionSpec as P

MESH = pl.DeviceIdType.MESH
RING_X, RING_Z = 4, 8
SIDE = 256
BF16, F32 = jnp.bfloat16, jnp.float32


def position():
    param = lax.axis_index("param")
    z, x, core = param // 8, (param // 2) % 4, param % 2
    return z, x, core, lax.axis_index("tok"), lax.axis_index("probe")


def device(z, x, core, tok, probe):
    return ((z * RING_X + x) * 2 + core, tok, probe)


def wrap(value, size):
    return lax.rem(value + 2 * size, size)


def signed_table(width):
    rows = lax.broadcasted_iota(jnp.int32, (width, width), 0)
    cols = lax.broadcasted_iota(jnp.int32, (width, width), 1)
    bits = rows & cols
    bits = bits ^ (bits >> 4)
    bits = bits ^ (bits >> 2)
    bits = bits ^ (bits >> 1)
    return (1 - 2 * (bits & 1)).astype(F32).astype(BF16)


def split_two(value):
    high = value.astype(BF16)
    return high, (value - high.astype(F32)).astype(BF16)


def butterfly(values):
    values = list(values)
    gap = 1
    while gap < len(values):
        for start in range(0, len(values), 2 * gap):
            for i in range(start, start + gap):
                a, b = values[i], values[i + gap]
                values[i], values[i + gap] = a + b, a - b
        gap *= 2
    return values


def transform_kernel(
    x_ref, ct_ref, signs_ref, out_ref,
    xh, xfb, zfb, xf, zf, sg, ct_raw, ct_send, ct_land, ct_own, ct_other, table,
    xo, base, sign_t, f_own, f_sib, local_sem, send_sem, recv_sem,
):
    z, x, core, tok, probe = position()
    half = 4096
    near = device(z, x, core, 1 - tok, probe)
    far = device(z, x, core, 1 - tok, 1 - probe)
    right_x = device(z, wrap(x + 1, RING_X), core, tok, probe)
    left_x = device(z, wrap(x - 1, RING_X), core, tok, probe)
    right_z = device(wrap(z + 1, RING_Z), x, core, tok, probe)
    left_z = device(wrap(z - 1, RING_Z), x, core, tok, probe)
    sibling = device(z, x, 1 - core, tok, probe)

    mine = pl.multiple_of(tok * half, 128)
    theirs = pl.multiple_of((1 - tok) * half + core * 2048, 128)
    loads = [
        pltpu.make_async_copy(ct_ref, ct_raw, local_sem.at[0]),
        pltpu.make_async_copy(
            x_ref.at[pl.ds(pl.multiple_of(64 * z, 64), 64), pl.ds(theirs + 1024, 1024)], zfb, local_sem.at[1]),
        pltpu.make_async_copy(
            x_ref.at[pl.ds(pl.multiple_of(128 * x, 128), 128), pl.ds(theirs, 1024)], xfb, local_sem.at[2]),
        pltpu.make_async_copy(x_ref.at[:, pl.ds(mine, half)], xh, local_sem.at[3]),
        pltpu.make_async_copy(signs_ref, sg, local_sem.at[4]),
    ]
    for load in loads:
        load.start()

    barrier = pltpu.get_barrier_semaphore()
    for other in (near, far, right_x, left_x, right_z, left_z, sibling):
        pl.semaphore_signal(barrier, inc=1, device_id=other, device_id_type=MESH)

    numbers = {}
    sent = []

    def number(name):
        return numbers.setdefault(name, len(numbers))

    def send(name, src, dst, target):
        n = number(name)
        copy = pltpu.make_async_remote_copy(
            src_ref=src, dst_ref=dst, send_sem=send_sem.at[n], recv_sem=recv_sem.at[n],
            device_id=target, device_id_type=MESH)
        copy.start()
        sent.append(copy)

    def arrived(name, dst, source):
        n = number(name)
        pltpu.make_async_remote_copy(
            src_ref=dst, dst_ref=dst, send_sem=send_sem.at[n], recv_sem=recv_sem.at[n],
            device_id=source, device_id_type=MESH).wait_recv()

    def xs(j, i):
        return xo.at[core * 8 + j, pl.ds(pl.multiple_of(128 * wrap(i, RING_X), 128), 128)]

    def zs(j, i):
        return xo.at[core * 8 + 4 + j, pl.ds(pl.multiple_of(64 * wrap(i, RING_Z), 64), 64)]

    loads[0].wait()
    ct_send[...] = ct_raw[...].astype(F32)
    loads[1].wait()
    for j in range(4):
        zf[j] = zfb[:, j * SIDE:(j + 1) * SIDE].astype(F32)
    loads[2].wait()
    for j in range(4):
        xf[j] = xfb[:, j * SIDE:(j + 1) * SIDE].astype(F32)
    pl.semaphore_wait(barrier, 7)

    send("ct", ct_send, ct_land, near)
    route = [far, far, far, near]
    for j in range(4):
        send(("zy", j), zf.at[j], zs(j, z), route[j])
        send(("xy", j), xf.at[j], xs(j, x), route[j])

    table[...] = signed_table(SIDE)
    ct_own[...] = jnp.zeros_like(ct_own)
    ct_other[...] = jnp.zeros_like(ct_other)
    ct_own[0:224, :] = ct_raw[...]
    loads[3].wait()
    loads[4].wait()

    def prepare(first):
        def body(i, carry):
            g = first + i
            even = sg[pl.ds(pl.multiple_of(512 * g, 512), SIDE, stride=2), :]
            odd = sg[pl.ds(pl.multiple_of(512 * g, 512) + 1, SIDE, stride=2), :]
            turned = jnp.concatenate([even.astype(F32).T, odd.astype(F32).T], axis=0)
            product = jnp.dot(
                ct_own[...], xh[:, pl.ds(pl.multiple_of(SIDE * g, SIDE), SIDE)], preferred_element_type=F32)
            sign_t[g] = turned
            base[g] = turned * product
            return carry

        lax.fori_loop(0, 4, body, 0)

    def process(g):
        h = table[...]
        product = jnp.dot(ct_other[...], xo[g].astype(BF16), preferred_element_type=F32)
        high, low = split_two(base[g] + sign_t[g] * product)
        mixed = jnp.dot(h, high, preferred_element_type=F32) + jnp.dot(h, low, preferred_element_type=F32)
        high, low = split_two(mixed)
        mixed = jnp.dot(high, h, preferred_element_type=F32) + jnp.dot(low, h, preferred_element_type=F32)
        f_own[2 * g] = mixed[:, 0:128]
        f_own[2 * g + 1] = mixed[:, 128:256]

    def process_mine(k):
        g = core * 8 + k
        process(g)
        send(("f0", k), f_own.at[pl.ds(2 * g, 2)], f_sib.at[pl.ds(2 * g, 2)], sibling)

    def process_theirs(k):
        g = (1 - core) * 8 + k
        arrived(("share", k), xo.at[g], sibling)
        process(g)
        send(("f1", k), f_own.at[pl.ds(2 * g, 2)], f_sib.at[pl.ds(2 * g, 2)], sibling)

    def take_ct():
        arrived("ct", ct_land, near)
        ct_other[0:224, :] = ct_land[...].astype(BF16)

    def complete(k):
        g = core * 8 + k
        send(("share", k), xo.at[g], xo.at[g], sibling)

    def x0(j):
        arrived(("xy", j), xs(j, x), route[j])
        send(("xr", j), xs(j, x), xs(j, x), right_x)
        send(("xl", j), xs(j, x), xs(j, x), left_x)

    def x1(j):
        arrived(("xr", j), xs(j, x - 1), left_x)
        if j % 2 == 0:
            send(("xe", j), xs(j, x - 1), xs(j, x - 1), right_x)
        arrived(("xl", j), xs(j, x + 1), right_x)
        if j % 2 == 1:
            send(("xe", j), xs(j, x + 1), xs(j, x + 1), left_x)

    def x2(j):
        arrived(("xe", j), xs(j, x + 2), left_x if j % 2 == 0 else right_x)
        complete(j)

    def z0(j):
        arrived(("zy", j), zs(j, z), route[j])
        send(("zr", j, 1), zs(j, z), zs(j, z), right_z)
        send(("zl", j, 1), zs(j, z), zs(j, z), left_z)

    def zh(j, d):
        arrived(("zr", j, d), zs(j, z - d), left_z)
        if d < 3 or j % 2 == 0:
            send(("zr", j, d + 1), zs(j, z - d), zs(j, z - d), right_z)
        arrived(("zl", j, d), zs(j, z + d), right_z)
        if d < 3 or j % 2 == 1:
            send(("zl", j, d + 1), zs(j, z + d), zs(j, z + d), left_z)

    def z4(j):
        if j % 2 == 0:
            arrived(("zr", j, 4), zs(j, z - 4), left_z)
        else:
            arrived(("zl", j, 4), zs(j, z + 4), right_z)
        complete(4 + j)

    steps = [(0.5 + 1.5 * i, functools.partial(prepare, 4 * i)) for i in range(4)]
    steps.append((9.9, take_ct))
    for j in range(4):
        at = 4.2 + 4.2 * j
        done = at + 4.2
        steps += [(at, functools.partial(x0, j)), (at + 2.5, functools.partial(x1, j)), (done, functools.partial(x2, j))]
        steps += [(max(done, 10.0) + 0.1, functools.partial(process_mine, j)),
                  (max(done, 10.0) + 1.5, functools.partial(process_theirs, j))]
        at = 1.4 + 4.9 * j
        done = at + 6.4
        steps.append((at, functools.partial(z0, j)))
        steps += [(at + 1.6 * d, functools.partial(zh, j, d)) for d in (1, 2, 3)]
        steps.append((done, functools.partial(z4, j)))
        steps += [(max(done, 10.0) + 0.1, functools.partial(process_mine, 4 + j)),
                  (max(done, 10.0) + 1.5, functools.partial(process_theirs, 4 + j))]
    for _, step in sorted(steps, key=lambda entry: entry[0]):
        step()

    for k in range(8):
        g = (1 - core) * 8 + k
        arrived(("f0", k), f_sib.at[pl.ds(2 * g, 2)], sibling)
        g = core * 8 + k
        arrived(("f1", k), f_sib.at[pl.ds(2 * g, 2)], sibling)

    flip = (1 - 2 * core).astype(F32)

    def last(i, carry):
        part, row = i // 32, pl.multiple_of((i % 32) * 8, 8)
        own = [f_own[2 * g + part, pl.ds(row, 8), :] for g in range(16)]
        sib = [f_sib[2 * g + part, pl.ds(row, 8), :] for g in range(16)]
        plus = butterfly([a + b for a, b in zip(own, sib)])
        minus = butterfly([(a - b) * flip for a, b in zip(own, sib)])
        for g in range(16):
            out_ref[0, 2 * g + part, pl.ds(row, 8), :] = plus[g]
            out_ref[1, 2 * g + part, pl.ds(row, 8), :] = minus[g]
        return carry

    lax.fori_loop(0, 64, last, 0)
    for copy in sent:
        copy.wait_send()


def transform(tokens_x, cot_t, signs):
    copies = 96
    return pl.pallas_call(
        transform_kernel,
        out_shape=jax.ShapeDtypeStruct((2, 32, SIDE, 128), F32),
        in_specs=[pl.BlockSpec(memory_space=pl.ANY)] * 3,
        out_specs=pl.BlockSpec(memory_space=pltpu.VMEM),
        scratch_shapes=[
            pltpu.VMEM((512, 4096), BF16),
            pltpu.VMEM((128, 1024), BF16),
            pltpu.VMEM((64, 1024), BF16),
            pltpu.VMEM((4, 128, SIDE), F32),
            pltpu.VMEM((4, 64, SIDE), F32),
            pltpu.VMEM((8192, 128), jnp.int32),
            pltpu.VMEM((224, 512), BF16),
            pltpu.VMEM((224, 512), F32),
            pltpu.VMEM((224, 512), F32),
            pltpu.VMEM((SIDE, 512), BF16),
            pltpu.VMEM((SIDE, 512), BF16),
            pltpu.VMEM((SIDE, SIDE), BF16),
            pltpu.VMEM((16, 512, SIDE), F32),
            pltpu.VMEM((16, SIDE, SIDE), F32),
            pltpu.VMEM((16, SIDE, SIDE), F32),
            pltpu.VMEM((32, SIDE, 128), F32),
            pltpu.VMEM((32, SIDE, 128), F32),
            pltpu.SemaphoreType.DMA((5,)),
            pltpu.SemaphoreType.DMA((copies,)),
            pltpu.SemaphoreType.DMA((copies,)),
        ],
        compiler_params=pltpu.CompilerParams(
            collective_id=0, has_side_effects=True, vmem_limit_bytes=50 << 20),
        cost_estimate=pl.CostEstimate(flops=8 << 30, bytes_accessed=24 << 20, transcendentals=0),
        name="transform",
    )(tokens_x, cot_t, signs)


def sketch_kernel(
    index_ref, samples_ref, t_ref, sketch_ref, basis_ref,
    rows, mine, land_xt, red, land_z, full, send_sem, recv_sem,
):
    z, x, core, tok, probe = position()
    lane_mates = [((i // 2), i % 2) for i in range(1, 8)]
    me = x * 2 + tok

    def xt_device(member):
        return device(z, member // 2, core, member % 2, probe)

    group = [(dx, dt, dp, dc) for dx in range(4) for dt in range(2) for dp in range(2) for dc in range(2)][1:]

    def group_device(offset):
        dx, dt, dp, dc = offset
        return device(z, wrap(x + dx, RING_X), core ^ dc, tok ^ dt, probe ^ dp)

    def group_source(offset):
        dx, dt, dp, dc = offset
        return wrap(x - dx, RING_X), core ^ dc, tok ^ dt, probe ^ dp

    barrier = pltpu.get_barrier_semaphore()
    for offset in group:
        pl.semaphore_signal(barrier, inc=1, device_id=group_device(offset), device_id_type=MESH)
    for d in range(1, 8):
        pl.semaphore_signal(
            barrier, inc=1, device_id=device(wrap(z + d, RING_Z), x, core, tok, probe), device_id_type=MESH)

    code = tok | (x << 2) | (z << 4)
    lanes = lax.broadcasted_iota(jnp.int32, (128, 128), 0)

    def gather_piece(piece):
        row0 = core * 64 + piece * 8

        def body(b, carry):
            row = row0 + b
            for k in range(128):
                rows[k:k + 1, :] = t_ref[pl.ds(index_ref[row * 128 + k], 1), :]
            m = samples_ref[pl.ds(row, 1), :]
            picked = jnp.where(lanes == ((m >> 8) & 127), rows[...].T, 0.0)
            value = jnp.sum(picked, axis=0, keepdims=True)
            odd = (m >> 20) & code
            odd = odd ^ (odd >> 4)
            odd = odd ^ (odd >> 2)
            odd = odd ^ (odd >> 1)
            mine[piece, pl.ds(b, 1), :] = jnp.where((odd & 1) == 1, -value, value)
            return carry

        lax.fori_loop(0, 8, body, 0)

    sent = []
    for d in range(1, 8):
        piece = wrap(me + d, 8)
        gather_piece(piece)
        if d == 1:
            pl.semaphore_wait(barrier, 38)
        copy = pltpu.make_async_remote_copy(
            src_ref=mine.at[piece], dst_ref=land_xt.at[d - 1], send_sem=send_sem.at[d - 1],
            recv_sem=recv_sem.at[d - 1], device_id=xt_device(piece), device_id_type=MESH)
        copy.start()
        sent.append(copy)
    gather_piece(me)
    total = mine[me]
    for d in range(1, 8):
        pltpu.make_async_remote_copy(
            src_ref=land_xt.at[d - 1], dst_ref=land_xt.at[d - 1], send_sem=send_sem.at[d - 1],
            recv_sem=recv_sem.at[d - 1], device_id=xt_device(wrap(me - d, 8)), device_id_type=MESH).wait_recv()
        total = total + land_xt[d - 1]
    red[...] = total

    def z_copy(source, target):
        return pltpu.make_async_remote_copy(
            src_ref=red, dst_ref=land_z.at[source], send_sem=send_sem.at[7 + target],
            recv_sem=recv_sem.at[7 + source], device_id=device(target, x, core, tok, probe), device_id_type=MESH)

    for d in range(1, 8):
        copy = z_copy(z, wrap(z + d, RING_Z))
        copy.start()
        sent.append(copy)
    land_z[z] = total
    for d in range(1, 8):
        z_copy(wrap(z - d, RING_Z), z).wait_recv()
    total = land_z[0]
    for i in range(1, 8):
        total = total + land_z[i]
    scale = float(1024 * 134217728) ** (-0.5)

    def place(px, pcore, ptok, pprobe):
        return full.at[pprobe, pl.ds(pl.multiple_of(pcore * 64 + (px * 2 + ptok) * 8, 8), 8)]

    here = place(x, core, tok, probe)
    here[...] = total * scale
    for i, offset in enumerate(group):
        copy = pltpu.make_async_remote_copy(
            src_ref=here, dst_ref=here, send_sem=send_sem.at[15 + i], recv_sem=recv_sem.at[15 + i],
            device_id=group_device(offset), device_id_type=MESH)
        copy.start()
        sent.append(copy)
    for i, offset in enumerate(group):
        px, pcore, ptok, pprobe = group_source(offset)
        there = place(px, pcore, ptok, pprobe)
        pltpu.make_async_remote_copy(
            src_ref=there, dst_ref=there, send_sem=send_sem.at[15 + i], recv_sem=recv_sem.at[15 + i],
            device_id=device(z, px, pcore, ptok, pprobe), device_id_type=MESH).wait_recv()

    count = 16384.0

    def mean(value):
        return jnp.sum(jnp.sum(value, axis=0, keepdims=True), axis=1, keepdims=True) / count

    first, second = full[0], full[1]
    unit = first * lax.rsqrt(mean(first * first) + 1e-06)
    rest = second - mean(unit * second) * unit
    last = rest * lax.rsqrt(mean(rest * rest) + 1e-06)
    rows[...] = unit
    land_rest = land_z
    start = pl.multiple_of(probe * 64, 64)
    for i in range(64):
        cols = slice(i * 128, (i + 1) * 128)
        sketch_ref[0:1, cols] = full[0, pl.ds(start + i, 1), :]
        sketch_ref[1:2, cols] = full[1, pl.ds(start + i, 1), :]
        basis_ref[0:1, cols] = rows[pl.ds(start + i, 1), :]
    rows[...] = last
    for i in range(64):
        basis_ref[1:2, i * 128:(i + 1) * 128] = rows[pl.ds(start + i, 1), :]
    for copy in sent:
        copy.wait_send()


def sketch(samples, table):
    index = ((samples >> 21 & 1) << 13) | ((samples >> 15 & 31) << 8) | (samples & 255)
    shape = jax.ShapeDtypeStruct((2, 8192), F32)
    return pl.pallas_call(
        sketch_kernel,
        out_shape=(shape, shape),
        in_specs=[
            pl.BlockSpec(memory_space=pltpu.SMEM),
            pl.BlockSpec(memory_space=pltpu.VMEM),
            pl.BlockSpec(memory_space=pltpu.VMEM),
        ],
        out_specs=(pl.BlockSpec(memory_space=pltpu.VMEM), pl.BlockSpec(memory_space=pltpu.VMEM)),
        scratch_shapes=[
            pltpu.VMEM((128, 128), F32),
            pltpu.VMEM((8, 8, 128), F32),
            pltpu.VMEM((7, 8, 128), F32),
            pltpu.VMEM((8, 128), F32),
            pltpu.VMEM((8, 8, 128), F32),
            pltpu.VMEM((2, 128, 128), F32),
            pltpu.SemaphoreType.DMA((46,)),
            pltpu.SemaphoreType.DMA((46,)),
        ],
        compiler_params=pltpu.CompilerParams(
            collective_id=1, has_side_effects=True, vmem_limit_bytes=24 << 20),
        cost_estimate=pl.CostEstimate(flops=1 << 24, bytes_accessed=8 << 20, transcendentals=0),
        name="sketch",
    )(index, samples.reshape(128, 128), table)


def on_device(tokens_x, cotangent, signs, samples):
    table = transform(tokens_x, cotangent[0].T, signs.reshape(8192, 128))
    return sketch(samples, table.reshape(16384, 128))


def solution(mesh):
    in_specs = (P("tok", None), P("probe", "tok", "param"), P(("param", "tok")), P())
    out_specs = (P(None, "probe"), P(None, "probe"))
    return jax.shard_map(
        on_device, mesh=mesh, in_specs=in_specs, out_specs=out_specs, check_vma=False
    )
```

time: 1460 us -> 113 us (0.08)
  waiting for transfers between devices: 1130 us -> 0 us
  local copies, waits for them, and re-layouts: 224 us -> 5.57 us
  Pallas kernels: 0 us -> 106 us
  matrix products: 33.4 us -> 0 us
  blocking collectives: 25.4 us -> 0 us
  between operations: 17.5 us -> 0.67 us
    psum x1 -> x0, waiting for transfers between devices: 923 us -> none  [on_device(): sketch_row = lax.psum(values, ('param', 'tok'))]
    gather x1 -> x0, local copies, waits for them, and re-layouts: 192 us -> none  [on_device(): values = jnp.where(owned, jnp.take(finished.reshape(-1), position), 0.0)]
    reduce_scatter x1 -> x0, waiting for transfers between devices: 108 us -> none  [on_device(): lax.psum_scatter(jnp.pad(product, ((0, 0), (0, pad_width - col_count))),...]
    pallas_call x0 -> x2, Pallas kernels: none -> 106 us  [the longest x1 75.3 us: transform(): pl.pallas_call(transform_kernel, out_shape=jax.ShapeDtypeStruct((2, 32, S...]
    all_to_all x1 -> x0, waiting for transfers between devices: 96.2 us -> none  [on_device(): lax.all_to_all(mixed.reshape(group_size, block_len), ('param', 'tok'), sp...]
    dot_general x5 -> x0, matrix products: 33.4 us -> none  [the longest x2 15.4 us: hadamard(): jnp.einsum('fg,agb->afb', table, shaped, precision=lax.Precision.HIGHEST)]
    psum x3 -> x0, blocking collectives: 17.4 us -> none  [the longest x1 5.8 us: on_device(): mean_first = lax.psum(jnp.sum(first * first) / total_rows, 'probe') + 1e-06]
  transfers between devices with their start and end apart: 3 -> 0, of which waited for: 3 -> 0; matrix products, arithmetic and copies ran while one was open for 0% -> 0% of each run, Pallas kernels for 0% -> 0%
where the time goes in v1:
time: 113 us
  Pallas kernels  106 us (94%)
  local copies, waits for them, and re-layouts  5.57 us (5%)
    pallas_call x1, Pallas kernels, transform(): pl.pallas_call(transform_kernel, out_shape=jax.ShapeDtypeStruct((2, 32, S...  75.3 us
    pallas_call x1, Pallas kernels, sketch(): pl.pallas_call(sketch_kernel, out_shape=(shape, shape), in_specs=[pl.Bloc...  30.2 us
    unnamed x8, local copies, waits for them, and re-layouts  5.57 us

profile of v1, /device:TPU:1, one launch (start us, length us, event | category | flops | bytes accessed | tf_op | source)
XLA Modules:
  0.0 112.6 jit_solution(6663801799848119091)
XLA Ops:
  0.6 0.9 and_or_fusion.index_ref
  1.5 0.0 copy-start.2
  1.5 0.9 copy-done.2
  2.4 0.0 copy-start.1
  2.4 75.3 %transform.1 = f32[2,32,256,128]{3,2,1,0:T(8,128)} custom-call(bf16[512,8192]{1,0:T(8,128)(2,1)} %x_ref.1, bf16[224,512]{1,0:T(8,128)(2,1)S(1)} %bitcast.8, s32[8192,128]{1,0:T(8,128)} %bitcast.9), custom_call_target="tpu_custom_call" | custom-call | flops 8589934592 | bytes 25165824 | tf_op jit(solution)/shard_map/transform/pallas_call | solution.py:263
  77.7 0.0 copy-done.1
  77.7 0.0 copy-start
  77.7 3.4 %copy-done = f32[2,32,256,128]{3,2,1,0:T(8,128)S(1)} copy-done((f32[2,32,256,128]{3,2,1,0:T(8,128)S(1)}, f32[2,32,256,128]{3,2,1,0:T(8,128)}, u32[]{:S(2)}) %copy-start) | copy-done | bytes 8388632
  81.1 30.2 %sketch.1 = (f32[2,8192]{1,0:T(2,128)S(1)}, f32[2,8192]{1,0:T(2,128)S(1)}) custom-call(s32[16384]{0:T(1024)S(1)} %and_or_fusion.index_ref, s32[128,128]{1,0:T(8,128)S(1)} %bitcast.7, f32[16384,128]{1,0:T(8,128)S(1)} %bitcast.6), custom_call_target="tpu_custom_call" | custom-call | flops 16777216 | bytes 8388608 | tf_op jit(solution)/shard_map/sketch/pallas_call | solution.py:429
  111.4 0.6 copy.8
  112.0 0.6 copy.9
Async XLA Ops:
  1.5 0.9 copy-start.2
  2.4 75.3 %copy-start.1 = (s32[16384]{0:T(1024)S(1)}, s32[16384]{0:T(1024)}, u32[]{:S(2)}) copy-start(s32[16384]{0:T(1024)} %param.7) | copy-start | bytes 196612
  77.7 3.4 %copy-start = (f32[2,32,256,128]{3,2,1,0:T(8,128)S(1)}, f32[2,32,256,128]{3,2,1,0:T(8,128)}, u32[]{:S(2)}) copy-start(f32[2,32,256,128]{3,2,1,0:T(8,128)} %transform.1) | copy-start | bytes 25165828

commit v2 on v1

v2 whole, which is shorter than its diff:
```python
import functools

import jax
import jax.numpy as jnp
from jax import lax
from jax.experimental import pallas as pl
from jax.experimental.pallas import tpu as pltpu
from jax.sharding import PartitionSpec as P

MESH = pl.DeviceIdType.MESH
RING_X, RING_Z = 4, 8
SIDE = 256
BF16, F32 = jnp.bfloat16, jnp.float32


def position():
    param = lax.axis_index("param")
    z, x, core = param // 8, (param // 2) % 4, param % 2
    return z, x, core, lax.axis_index("tok"), lax.axis_index("probe")


def device(z, x, core, tok, probe):
    return ((z * RING_X + x) * 2 + core, tok, probe)


def wrap(value, size):
    return lax.rem(value + 2 * size, size)


def signed_table(width):
    rows = lax.broadcasted_iota(jnp.int32, (width, width), 0)
    cols = lax.broadcasted_iota(jnp.int32, (width, width), 1)
    bits = rows & cols
    bits = bits ^ (bits >> 4)
    bits = bits ^ (bits >> 2)
    bits = bits ^ (bits >> 1)
    return (1 - 2 * (bits & 1)).astype(F32).astype(BF16)


def split_two(value):
    high = value.astype(BF16)
    return high, (value - high.astype(F32)).astype(BF16)


def butterfly(values):
    values = list(values)
    gap = 1
    while gap < len(values):
        for start in range(0, len(values), 2 * gap):
            for i in range(start, start + gap):
                a, b = values[i], values[i + gap]
                values[i], values[i + gap] = a + b, a - b
        gap *= 2
    return values


FEED = (("f", 5), ("n", 2), ("f", 4), ("n", 3), ("f", 6), ("n", "ct"), ("f", 0), ("n", 7), ("f", 1), ("f", 7))
ORDER = (
    "p00 p10 p20 p30", "z50 z40 x20 z60", "z51 x30 z41 x00", "z61 x21 z52 x10", "z42 x31 z62 z53",
    "x01 z43 c00 z63", "x22 m20 z54 m50", "z44 m40 t20 x32", "x11 m30 z64 t50", "m60 t40 y70 t30",
    "x02 m70 m00 t60", "q20 x12 t70 m10", "t00 q10 t10 q30", "q00",
)


def whole_kernel(
    x_ref, ct_ref, signs_ref, samples_ref, sketch_ref, basis_ref,
    xh, xfb, zfb, yfb, xf, zf, yf, sg, ct_raw, ct_send, ct_land, ct_own, ct_other, table,
    xo, base, sign_t, f_own, f_sib, grid, samples, index_v, index_s,
    rows, mine, land_xt, red, land_z, full,
    local_sem, send_sem, recv_sem, send_small, recv_small,
):
    z, x, core, tok, probe = position()
    half = 4096
    near = device(z, x, core, 1 - tok, probe)
    far = device(z, x, core, 1 - tok, 1 - probe)
    right_x = device(z, wrap(x + 1, RING_X), core, tok, probe)
    left_x = device(z, wrap(x - 1, RING_X), core, tok, probe)
    right_z = device(wrap(z + 1, RING_Z), x, core, tok, probe)
    left_z = device(wrap(z - 1, RING_Z), x, core, tok, probe)
    sibling = device(z, x, 1 - core, tok, probe)
    group = [(dx, dt, dp, dc) for dx in range(4) for dt in range(2) for dp in range(2) for dc in range(2)][1:]

    def group_device(offset):
        dx, dt, dp, dc = offset
        return device(z, wrap(x + dx, RING_X), core ^ dc, tok ^ dt, probe ^ dp)

    mine_at = pl.multiple_of(tok * half, 128)
    theirs = pl.multiple_of((1 - tok) * half + core * 2048, 128)
    loads = [
        pltpu.make_async_copy(
            x_ref.at[pl.ds(pl.multiple_of(64 * z, 64), 64), pl.ds(theirs + 1024, 768)], zfb, local_sem.at[0]),
        pltpu.make_async_copy(
            x_ref.at[pl.ds(pl.multiple_of(128 * x, 128), 128), pl.ds(theirs, 1024)], xfb, local_sem.at[1]),
        pltpu.make_async_copy(ct_ref, ct_raw, local_sem.at[2]),
        pltpu.make_async_copy(x_ref.at[:, pl.ds(theirs + 1792, SIDE)], yfb, local_sem.at[3]),
        pltpu.make_async_copy(samples_ref, samples, local_sem.at[4]),
        pltpu.make_async_copy(x_ref.at[:, pl.ds(mine_at, half)], xh, local_sem.at[5]),
        pltpu.make_async_copy(signs_ref, sg, local_sem.at[6]),
    ]
    for load in loads:
        load.start()

    barrier = pltpu.get_barrier_semaphore()
    for d in range(1, 8):
        pl.semaphore_signal(
            barrier, inc=1, device_id=device(wrap(z + d, RING_Z), x, core, tok, probe), device_id_type=MESH)
    for offset in group:
        pl.semaphore_signal(barrier, inc=1, device_id=group_device(offset), device_id_type=MESH)

    numbers = {}
    sent = []

    def number(name):
        return numbers.setdefault(name, len(numbers))

    def send(name, src, dst, target):
        n = number(name)
        copy = pltpu.make_async_remote_copy(
            src_ref=src, dst_ref=dst, send_sem=send_sem.at[n], recv_sem=recv_sem.at[n],
            device_id=target, device_id_type=MESH)
        copy.start()
        sent.append(copy)

    def arrived(name, dst, source):
        n = number(name)
        pltpu.make_async_remote_copy(
            src_ref=dst, dst_ref=dst, send_sem=send_sem.at[n], recv_sem=recv_sem.at[n],
            device_id=source, device_id_type=MESH).wait_recv()

    def xs(k, i):
        return xo.at[core * 8 + k, pl.ds(pl.multiple_of(128 * wrap(i, RING_X), 128), 128)]

    def zs(k, i):
        return xo.at[core * 8 + k, pl.ds(pl.multiple_of(64 * wrap(i, RING_Z), 64), 64)]

    loads[0].wait()
    for j in range(3):
        zf[j] = zfb[:, j * SIDE:(j + 1) * SIDE].astype(F32)
    loads[1].wait()
    for j in range(4):
        xf[j] = xfb[:, j * SIDE:(j + 1) * SIDE].astype(F32)
    loads[2].wait()
    ct_send[...] = ct_raw[...].astype(F32)
    loads[3].wait()
    yf[...] = yfb[...].astype(F32)
    pl.semaphore_wait(barrier, 38)

    route = {}
    for side, k in FEED:
        target = near if side == "n" else far
        if k == "ct":
            send("ct", ct_send, ct_land, target)
        elif k == 7:
            part = pl.ds(0 if side == "n" else 256, 256)
            send(("feed", 7, side), yf.at[part], xo.at[core * 8 + 7, part], target)
        else:
            route[k] = target
            if k < 4:
                send(("feed", k), xf.at[k], xs(k, x), target)
            else:
                send(("feed", k), zf.at[k - 4], zs(k, z), target)

    table[...] = signed_table(SIDE)
    ct_own[...] = jnp.zeros_like(ct_own)
    ct_other[...] = jnp.zeros_like(ct_other)
    ct_own[0:224, :] = ct_raw[...]
    loads[4].wait()
    m = samples[pl.ds(pl.multiple_of(core * 64, 64), 64), :]
    index_v[...] = ((m >> 21 & 1) << 13) | ((m >> 15 & 31) << 8) | (m & 255)
    to_scalar = pltpu.make_async_copy(index_v, index_s, local_sem.at[7])
    to_scalar.start()
    loads[5].wait()
    loads[6].wait()

    def prepare(part):
        def body(i, carry):
            g = 4 * part + i
            even = sg[pl.ds(pl.multiple_of(512 * g, 512), SIDE, stride=2), :]
            odd = sg[pl.ds(pl.multiple_of(512 * g, 512) + 1, SIDE, stride=2), :]
            turned = jnp.concatenate([even.astype(F32).T, odd.astype(F32).T], axis=0)
            product = jnp.dot(
                ct_own[...], xh[:, pl.ds(pl.multiple_of(SIDE * g, SIDE), SIDE)], preferred_element_type=F32)
            sign_t[g] = turned
            base[g] = turned * product
            return carry

        lax.fori_loop(0, 4, body, 0)

    def process(g):
        h = table[...]
        product = jnp.dot(ct_other[...], xo[g].astype(BF16), preferred_element_type=F32)
        high, low = split_two(base[g] + sign_t[g] * product)
        mixed = jnp.dot(h, high, preferred_element_type=F32) + jnp.dot(h, low, preferred_element_type=F32)
        high, low = split_two(mixed)
        mixed = jnp.dot(high, h, preferred_element_type=F32) + jnp.dot(low, h, preferred_element_type=F32)
        f_own[2 * g] = mixed[:, 0:128]
        f_own[2 * g + 1] = mixed[:, 128:256]

    def send_f(name, k, g):
        send((name, k), f_own.at[pl.ds(2 * g, 2)], f_sib.at[pl.ds(2 * g, 2)], sibling)

    def own_chunk(k):
        process(core * 8 + k)
        send_f("f0", k, core * 8 + k)

    def sibling_chunk(k):
        g = (1 - core) * 8 + k
        arrived(("share", k), xo.at[g], sibling)
        process(g)
        send_f("f1", k, g)

    flip = (1 - 2 * core).astype(F32)

    def quad(q):
        for k in (2 * q, 2 * q + 1):
            g = (1 - core) * 8 + k
            arrived(("f0", k), f_sib.at[pl.ds(2 * g, 2)], sibling)
            g = core * 8 + k
            arrived(("f1", k), f_sib.at[pl.ds(2 * g, 2)], sibling)
        blocks = [2 * q, 2 * q + 1, 8 + 2 * q, 9 + 2 * q]

        def body(i, carry):
            part, row = i // 16, pl.multiple_of((i % 16) * 16, 16)
            own = [f_own[2 * g + part, pl.ds(row, 16), :] for g in blocks]
            sib = [f_sib[2 * g + part, pl.ds(row, 16), :] for g in blocks]
            for core_bit in range(2):
                both = [a + b for a, b in zip(own, sib)] if core_bit == 0 else [(a - b) * flip for a, b in zip(own, sib)]
                for g, value in zip(blocks, butterfly(both)):
                    at = (core_bit * 32 + 2 * g + part) * SIDE + row
                    grid[pl.ds(pl.multiple_of(at, 16), 16), :] = value
            return carry

        lax.fori_loop(0, 32, body, 0, unroll=2)

    def take_ct():
        arrived("ct", ct_land, near)
        ct_other[0:224, :] = ct_land[...].astype(BF16)

    def complete(k):
        g = core * 8 + k
        send(("share", k), xo.at[g], xo.at[g], sibling)

    def hop_x(k, d):
        if d == 0:
            arrived(("feed", k), xs(k, x), route[k])
            send(("xr", k), xs(k, x), xs(k, x), right_x)
            send(("xl", k), xs(k, x), xs(k, x), left_x)
        elif d == 1:
            arrived(("xr", k), xs(k, x - 1), left_x)
            if k % 2 == 0:
                send(("xe", k), xs(k, x - 1), xs(k, x - 1), right_x)
            arrived(("xl", k), xs(k, x + 1), right_x)
            if k % 2 == 1:
                send(("xe", k), xs(k, x + 1), xs(k, x + 1), left_x)
        else:
            arrived(("xe", k), xs(k, x + 2), left_x if k % 2 == 0 else right_x)
            complete(k)

    def hop_z(k, d):
        if d == 0:
            arrived(("feed", k), zs(k, z), route[k])
            send(("zr", k, 1), zs(k, z), zs(k, z), right_z)
            send(("zl", k, 1), zs(k, z), zs(k, z), left_z)
        elif d < 4:
            arrived(("zr", k, d), zs(k, z - d), left_z)
            if d < 3 or k % 2 == 0:
                send(("zr", k, d + 1), zs(k, z - d), zs(k, z - d), right_z)
            arrived(("zl", k, d), zs(k, z + d), right_z)
            if d < 3 or k % 2 == 1:
                send(("zl", k, d + 1), zs(k, z + d), zs(k, z + d), left_z)
        else:
            if k % 2 == 0:
                arrived(("zr", k, 4), zs(k, z - 4), left_z)
            else:
                arrived(("zl", k, 4), zs(k, z + 4), right_z)
            complete(k)

    def hop_y(k):
        arrived(("feed", k, "n"), xo.at[core * 8 + k, pl.ds(0, 256)], near)
        arrived(("feed", k, "f"), xo.at[core * 8 + k, pl.ds(256, 256)], far)
        complete(k)

    for step in " ".join(ORDER).split():
        kind, k, d = step[0], int(step[1]), int(step[2])
        if kind == "x":
            hop_x(k, d)
        elif kind == "z":
            hop_z(k, d)
        elif kind == "y":
            hop_y(k)
        elif kind == "c":
            take_ct()
        elif kind == "p":
            prepare(k)
        elif kind == "m":
            own_chunk(k)
        elif kind == "t":
            sibling_chunk(k)
        else:
            quad(k)

    def last(i, carry):
        at = (i // 16) * 16 * SIDE + ((i // 4) % 4) * SIDE + (i % 4) * 64
        for r in range(0, 64, 16):
            places = [pl.ds(pl.multiple_of(at + q * 4 * SIDE + r, 16), 16) for q in range(4)]
            for place, value in zip(places, butterfly([grid[place, :] for place in places])):
                grid[place, :] = value
        return carry

    lax.fori_loop(0, 64, last, 0)
    to_scalar.wait()
    me = x * 2 + tok

    def xt_device(member):
        return device(z, member // 2, core, member % 2, probe)

    def group_source(offset):
        dx, dt, dp, dc = offset
        return wrap(x - dx, RING_X), core ^ dc, tok ^ dt, probe ^ dp

    code = tok | (x << 2) | (z << 4)
    lanes = lax.broadcasted_iota(jnp.int32, (128, 128), 0)

    def gather_piece(piece):
        row0 = core * 64 + piece * 8

        def body(b, carry):
            for k in range(128):
                rows[k:k + 1, :] = grid[pl.ds(index_s[piece * 8 + b, k], 1), :]
            m = samples[pl.ds(row0 + b, 1), :]
            picked = jnp.where(lanes == ((m >> 8) & 127), rows[...].T, 0.0)
            value = jnp.sum(picked, axis=0, keepdims=True)
            odd = (m >> 20) & code
            odd = odd ^ (odd >> 4)
            odd = odd ^ (odd >> 2)
            odd = odd ^ (odd >> 1)
            mine[piece, pl.ds(b, 1), :] = jnp.where((odd & 1) == 1, -value, value)
            return carry

        lax.fori_loop(0, 8, body, 0)

    for d in range(1, 8):
        piece = wrap(me + d, 8)
        gather_piece(piece)
        copy = pltpu.make_async_remote_copy(
            src_ref=mine.at[piece], dst_ref=land_xt.at[d - 1], send_sem=send_small.at[d - 1],
            recv_sem=recv_small.at[d - 1], device_id=xt_device(piece), device_id_type=MESH)
        copy.start()
        sent.append(copy)
    gather_piece(me)
    total = mine[me]
    for d in range(1, 8):
        pltpu.make_async_remote_copy(
            src_ref=land_xt.at[d - 1], dst_ref=land_xt.at[d - 1], send_sem=send_small.at[d - 1],
            recv_sem=recv_small.at[d - 1], device_id=xt_device(wrap(me - d, 8)), device_id_type=MESH).wait_recv()
        total = total + land_xt[d - 1]
    red[...] = total

    def z_copy(source, target):
        return pltpu.make_async_remote_copy(
            src_ref=red, dst_ref=land_z.at[source], send_sem=send_small.at[7 + target],
            recv_sem=recv_small.at[7 + source], device_id=device(target, x, core, tok, probe), device_id_type=MESH)

    for d in range(1, 8):
        copy = z_copy(z, wrap(z + d, RING_Z))
        copy.start()
        sent.append(copy)
    land_z[z] = total
    for d in range(1, 8):
        z_copy(wrap(z - d, RING_Z), z).wait_recv()
    total = land_z[0]
    for i in range(1, 8):
        total = total + land_z[i]
    scale = float(1024 * 134217728) ** (-0.5)

    def place(px, pcore, ptok, pprobe):
        return full.at[pprobe, pl.ds(pl.multiple_of(pcore * 64 + (px * 2 + ptok) * 8, 8), 8)]

    here = place(x, core, tok, probe)
    here[...] = total * scale
    for i, offset in enumerate(group):
        copy = pltpu.make_async_remote_copy(
            src_ref=here, dst_ref=here, send_sem=send_small.at[15 + i], recv_sem=recv_small.at[15 + i],
            device_id=group_device(offset), device_id_type=MESH)
        copy.start()
        sent.append(copy)
    for i, offset in enumerate(group):
        px, pcore, ptok, pprobe = group_source(offset)
        there = place(px, pcore, ptok, pprobe)
        pltpu.make_async_remote_copy(
            src_ref=there, dst_ref=there, send_sem=send_small.at[15 + i], recv_sem=recv_small.at[15 + i],
            device_id=device(z, px, pcore, ptok, pprobe), device_id_type=MESH).wait_recv()

    count = 16384.0

    def mean(value):
        return jnp.sum(jnp.sum(value, axis=0, keepdims=True), axis=1, keepdims=True) / count

    first, second = full[0], full[1]
    unit = first * lax.rsqrt(mean(first * first) + 1e-06)
    rest = second - mean(unit * second) * unit
    last = rest * lax.rsqrt(mean(rest * rest) + 1e-06)
    rows[...] = unit
    start = pl.multiple_of(probe * 64, 64)
    for i in range(64):
        cols = slice(i * 128, (i + 1) * 128)
        sketch_ref[0:1, cols] = full[0, pl.ds(start + i, 1), :]
        sketch_ref[1:2, cols] = full[1, pl.ds(start + i, 1), :]
        basis_ref[0:1, cols] = rows[pl.ds(start + i, 1), :]
    rows[...] = last
    for i in range(64):
        basis_ref[1:2, i * 128:(i + 1) * 128] = rows[pl.ds(start + i, 1), :]
    for copy in sent:
        copy.wait_send()


def whole(tokens_x, cot_t, signs, samples):
    shape = jax.ShapeDtypeStruct((2, 8192), F32)
    return pl.pallas_call(
        whole_kernel,
        out_shape=(shape, shape),
        in_specs=[pl.BlockSpec(memory_space=pl.ANY)] * 4,
        out_specs=(pl.BlockSpec(memory_space=pltpu.VMEM), pl.BlockSpec(memory_space=pltpu.VMEM)),
        scratch_shapes=[
            pltpu.VMEM((512, 4096), BF16),
            pltpu.VMEM((128, 1024), BF16),
            pltpu.VMEM((64, 768), BF16),
            pltpu.VMEM((512, SIDE), BF16),
            pltpu.VMEM((4, 128, SIDE), F32),
            pltpu.VMEM((3, 64, SIDE), F32),
            pltpu.VMEM((512, SIDE), F32),
            pltpu.VMEM((8192, 128), jnp.int32),
            pltpu.VMEM((224, 512), BF16),
            pltpu.VMEM((224, 512), F32),
            pltpu.VMEM((224, 512), F32),
            pltpu.VMEM((SIDE, 512), BF16),
            pltpu.VMEM((SIDE, 512), BF16),
            pltpu.VMEM((SIDE, SIDE), BF16),
            pltpu.VMEM((16, 512, SIDE), F32),
            pltpu.VMEM((16, SIDE, SIDE), F32),
            pltpu.VMEM((16, SIDE, SIDE), F32),
            pltpu.VMEM((32, SIDE, 128), F32),
            pltpu.VMEM((32, SIDE, 128), F32),
            pltpu.VMEM((16384, 128), F32),
            pltpu.VMEM((128, 128), jnp.int32),
            pltpu.VMEM((64, 128), jnp.int32),
            pltpu.SMEM((64, 128), jnp.int32),
            pltpu.VMEM((128, 128), F32),
            pltpu.VMEM((8, 8, 128), F32),
            pltpu.VMEM((7, 8, 128), F32),
            pltpu.VMEM((8, 128), F32),
            pltpu.VMEM((8, 8, 128), F32),
            pltpu.VMEM((2, 128, 128), F32),
            pltpu.SemaphoreType.DMA((8,)),
            pltpu.SemaphoreType.DMA((80,)),
            pltpu.SemaphoreType.DMA((80,)),
            pltpu.SemaphoreType.DMA((46,)),
            pltpu.SemaphoreType.DMA((46,)),
        ],
        compiler_params=pltpu.CompilerParams(
            collective_id=0, has_side_effects=True, vmem_limit_bytes=56 << 20),
        cost_estimate=pl.CostEstimate(flops=8 << 30, bytes_accessed=24 << 20, transcendentals=0),
        name="whole",
    )(tokens_x, cot_t, signs, samples)


def on_device(tokens_x, cotangent, signs, samples):
    return whole(tokens_x, cotangent[0].T, signs.reshape(8192, 128), samples.reshape(128, 128))


def solution(mesh):
    in_specs = (P("tok", None), P("probe", "tok", "param"), P(("param", "tok")), P())
    out_specs = (P(None, "probe"), P(None, "probe"))
    return jax.shard_map(
        on_device, mesh=mesh, in_specs=in_specs, out_specs=out_specs, check_vma=False
    )
```

time: 113 us -> 78.8 us (0.70)
  Pallas kernels: 106 us -> 75.1 us
  local copies, waits for them, and re-layouts: 5.57 us -> 2.95 us
    pallas_call x2 -> x1, Pallas kernels: 106 us -> 75.1 us  [whole(): pl.pallas_call(whole_kernel, out_shape=(shape, shape), in_specs=[pl.Block...]
    unnamed x8 -> x2, local copies, waits for them, and re-layouts: 5.57 us -> 2.95 us
where the time goes in v2:
time: 78.8 us; the launch traced here: 78.7 us
  Pallas kernels  75.1 us (95%)
  local copies, waits for them, and re-layouts  2.95 us (4%)
    pallas_call x1, Pallas kernels, whole(): pl.pallas_call(whole_kernel, out_shape=(shape, shape), in_specs=[pl.Block...  75.1 us
    unnamed x2, local copies, waits for them, and re-layouts  2.95 us

profile of v2, /device:TPU:1, one launch (start us, length us, event | category | flops | bytes accessed | tf_op | source)
XLA Modules:
  0.0 78.7 jit_solution(17873646123994319509)
XLA Ops:
  0.6 75.1 %whole.1 = (f32[2,8192]{1,0:T(2,128)}, f32[2,8192]{1,0:T(2,128)}) custom-call(bf16[512,8192]{1,0:T(8,128)(2,1)} %x_ref.1, bf16[224,512]{1,0:T(8,128)(2,1)} %bitcast.6, s32[8192,128]{1,0:T(8,128)} %bitcast.5, s32[128,128]{1,0:T(8,128)} %bitcast.7), custom_call_target="tpu_custom_call" | custom-call | flops 8589934592 | bytes 25165824 | tf_op jit(solution)/shard_map/whole/pallas_call | solution.py:419
  75.7 1.5 %copy.8 = f32[2,8192]{1,0:T(2,128)} copy(f32[2,8192]{1,0:T(2,128)} %get-tuple-element.4) | data formatting | bytes 131072
  77.2 1.5 %copy.9 = f32[2,8192]{1,0:T(2,128)} copy(f32[2,8192]{1,0:T(2,128)} %get-tuple-element.5) | data formatting | bytes 131072

commit v3 on v2

v3 whole, which is shorter than its diff:
```python
import functools

import jax
import jax.numpy as jnp
from jax import lax
from jax.experimental import pallas as pl
from jax.experimental.pallas import tpu as pltpu
from jax.sharding import PartitionSpec as P

MESH = pl.DeviceIdType.MESH
RING_X, RING_Z = 4, 8
SIDE = 256
BF16, F32 = jnp.bfloat16, jnp.float32


def position():
    param = lax.axis_index("param")
    z, x, core = param // 8, (param // 2) % 4, param % 2
    return z, x, core, lax.axis_index("tok"), lax.axis_index("probe")


def device(z, x, core, tok, probe):
    return ((z * RING_X + x) * 2 + core, tok, probe)


def wrap(value, size):
    return lax.rem(value + 2 * size, size)


def signed_table(width):
    rows = lax.broadcasted_iota(jnp.int32, (width, width), 0)
    cols = lax.broadcasted_iota(jnp.int32, (width, width), 1)
    bits = rows & cols
    bits = bits ^ (bits >> 4)
    bits = bits ^ (bits >> 2)
    bits = bits ^ (bits >> 1)
    return (1 - 2 * (bits & 1)).astype(F32).astype(BF16)


def split_two(value):
    high = value.astype(BF16)
    return high, (value - high.astype(F32)).astype(BF16)


def butterfly(values):
    values = list(values)
    gap = 1
    while gap < len(values):
        for start in range(0, len(values), 2 * gap):
            for i in range(start, start + gap):
                a, b = values[i], values[i + gap]
                values[i], values[i + gap] = a + b, a - b
        gap *= 2
    return values


FEED = (("n", 1), ("n", 5), ("f", 4), ("f", 2), ("n", "ct"), ("f", 6), ("f", 3), ("n", 7), ("f", 0), ("f", 7))
ORDER = (
    "z40 x10 z50 x20", "z41 z60 p00 z51", "x11 p10 x30 z42", "p20 z61 x21 p30", "x00 z52 z43 x12",
    "c00 z62 z53 x31", "x22 c10 m10 m20", "z44 m40 z63 x01", "z54 m50 y70 m70", "x32 m30 z64 m60",
    "q20 x02 m00 q10", "q30 q00",
)


def whole_kernel(
    x_ref, ct_ref, signs_ref, samples_ref, sketch_ref, basis_ref,
    xh, xfb, zfb, yfb, xf, zf, yf, sg, ct_raw, ct_send, ct_mate, ct_land, ct_own, ct_other, table,
    xo, base, sign_t, grid, samples, index_v, index_s,
    rows, rows_b, mine, land_xt, red, land_z, full,
    local_sem, send_sem, recv_sem, send_small, recv_small,
):
    z, x, core, tok, probe = position()
    half = 4096
    near = device(z, x, core, 1 - tok, probe)
    far = device(z, x, core, 1 - tok, 1 - probe)
    right_x = device(z, wrap(x + 1, RING_X), core, tok, probe)
    left_x = device(z, wrap(x - 1, RING_X), core, tok, probe)
    right_z = device(wrap(z + 1, RING_Z), x, core, tok, probe)
    left_z = device(wrap(z - 1, RING_Z), x, core, tok, probe)
    sibling = device(z, x, 1 - core, tok, probe)
    me = x * 2 + tok

    def xt_device(member):
        return device(z, member // 2, core, member % 2, probe)

    def column_device(other_z, other_core):
        return device(other_z, x, other_core, tok, probe)

    def plane_device(member, other_probe):
        return device(z, member // 2, core, member % 2, other_probe)

    column = [(dz, dc) for dz in range(8) for dc in range(2)][1:]
    plane = [(d, dp) for d in range(8) for dp in range(2)][1:]

    mine_at = pl.multiple_of(tok * half + core * 2048, 128)
    theirs = pl.multiple_of((1 - tok) * half + core * 2048, 128)
    loads = [
        pltpu.make_async_copy(
            x_ref.at[pl.ds(pl.multiple_of(64 * z, 64), 64), pl.ds(theirs + 1024, 768)], zfb, local_sem.at[0]),
        pltpu.make_async_copy(
            x_ref.at[pl.ds(pl.multiple_of(128 * x, 128), 128), pl.ds(theirs, 1024)], xfb, local_sem.at[1]),
        pltpu.make_async_copy(ct_ref, ct_raw, local_sem.at[2]),
        pltpu.make_async_copy(x_ref.at[:, pl.ds(theirs + 1792, SIDE)], yfb, local_sem.at[3]),
        pltpu.make_async_copy(samples_ref, samples, local_sem.at[4]),
        pltpu.make_async_copy(x_ref.at[:, pl.ds(mine_at, 2048)], xh, local_sem.at[5]),
        pltpu.make_async_copy(
            signs_ref.at[pl.ds(pl.multiple_of(core * half, half), half)], sg.at[core], local_sem.at[6]),
    ]
    for load in loads:
        load.start()

    barrier = pltpu.get_barrier_semaphore()
    partners = [plane_device(wrap(me + d, 8), probe ^ dp) for d, dp in plane]
    partners += [column_device(wrap(z + dz, 8), core ^ dc) for dz, dc in column]
    for partner in partners:
        pl.semaphore_signal(barrier, inc=1, device_id=partner, device_id_type=MESH)

    numbers = {}
    sent = []

    def number(name):
        return numbers.setdefault(name, len(numbers))

    def send(name, src, dst, target):
        n = number(name)
        copy = pltpu.make_async_remote_copy(
            src_ref=src, dst_ref=dst, send_sem=send_sem.at[n], recv_sem=recv_sem.at[n],
            device_id=target, device_id_type=MESH)
        copy.start()
        sent.append(copy)
        return copy

    def arrived(name, dst, source):
        n = number(name)
        pltpu.make_async_remote_copy(
            src_ref=dst, dst_ref=dst, send_sem=send_sem.at[n], recv_sem=recv_sem.at[n],
            device_id=source, device_id_type=MESH).wait_recv()

    def xs(k, i):
        return xo.at[k, pl.ds(pl.multiple_of(128 * wrap(i, RING_X), 128), 128)]

    def zs(k, i):
        return xo.at[k, pl.ds(pl.multiple_of(64 * wrap(i, RING_Z), 64), 64)]

    loads[0].wait()
    for j in range(3):
        zf[j] = zfb[:, j * SIDE:(j + 1) * SIDE].astype(F32)
    loads[1].wait()
    for j in range(4):
        xf[j] = xfb[:, j * SIDE:(j + 1) * SIDE].astype(F32)
    pl.semaphore_wait(barrier, len(partners))

    route = {}
    for side, k in FEED:
        target = near if side == "n" else far
        if k == "ct":
            loads[2].wait()
            ct_send[...] = ct_raw[...].astype(F32)
            send("ct", ct_send, ct_land.at[core], target)
        elif k == 7:
            if side == "n":
                loads[3].wait()
                yf[...] = yfb[...].astype(F32)
            part = pl.ds(0 if side == "n" else 256, 256)
            send(("feed", 7, side), yf.at[part], xo.at[7, part], target)
        else:
            route[k] = target
            if k < 4:
                send(("feed", k), xf.at[k], xs(k, x), target)
            else:
                send(("feed", k), zf.at[k - 4], zs(k, z), target)

    send("mate", ct_send, ct_mate, sibling)
    send("signs", signs_ref.at[pl.ds(pl.multiple_of((1 - core) * half, half), half)], sg.at[core], sibling)
    table[...] = signed_table(SIDE)
    ct_own[...] = jnp.zeros_like(ct_own)
    ct_other[...] = jnp.zeros_like(ct_other)
    own_rows = pl.ds(pl.multiple_of(core * SIDE, SIDE), 224)
    mate_rows = pl.ds(pl.multiple_of((1 - core) * SIDE, SIDE), 224)
    ct_own[own_rows, :] = ct_raw[...]
    loads[4].wait()
    m = samples[pl.ds(pl.multiple_of(core * 64, 64), 64), :]
    index_v[...] = ((m >> 16 & 15) << 10) | ((m >> 21 & 1) << 9) | ((m >> 15 & 1) << 8) | (m & 255)
    to_scalar = pltpu.make_async_copy(index_v, index_s, local_sem.at[7])
    to_scalar.start()
    loads[5].wait()
    loads[6].wait()
    arrived("mate", ct_mate, sibling)
    ct_own[mate_rows, :] = ct_mate[...].astype(BF16)
    arrived("signs", sg.at[1 - core], sibling)

    def prepare(part):
        def body(i, carry):
            k = 2 * part + i
            product = jnp.dot(
                ct_own[...], xh[:, pl.ds(pl.multiple_of(SIDE * k, SIDE), SIDE)], preferred_element_type=F32)
            for b in range(2):
                even = sg[b, pl.ds(pl.multiple_of(512 * k, 512), SIDE, stride=2), :]
                odd = sg[b, pl.ds(pl.multiple_of(512 * k, 512) + 1, SIDE, stride=2), :]
                turned = jnp.concatenate([even.astype(F32).T, odd.astype(F32).T], axis=0)
                rows_b = slice(b * SIDE, (b + 1) * SIDE)
                sign_t[k, rows_b, :] = turned
                base[k, rows_b, :] = turned * product[rows_b]
            return carry

        lax.fori_loop(0, 2, body, 0)

    def place_of(g, sel):
        return grid.at[pl.ds(pl.multiple_of(g * 1024 + sel * 512, 512), 512)]

    sent_grid = {}

    def process(k):
        h = table[...]
        product = jnp.dot(ct_other[...], xo[k].astype(BF16), preferred_element_type=F32)
        value = base[k] + sign_t[k] * product
        at = (core * 8 + k) * 1024
        for sel in range(2):
            both = value[:SIDE] + value[SIDE:] if sel == 0 else value[:SIDE] - value[SIDE:]
            high, low = split_two(both)
            mixed = jnp.dot(h, high, preferred_element_type=F32) + jnp.dot(h, low, preferred_element_type=F32)
            high, low = split_two(mixed)
            mixed = jnp.dot(high, h, preferred_element_type=F32) + jnp.dot(low, h, preferred_element_type=F32)
            for part in range(2):
                first_row = pl.multiple_of(at + (sel * 2 + part) * SIDE, SIDE)
                grid[pl.ds(first_row, SIDE), :] = mixed[:, part * 128:(part + 1) * 128]
            place = place_of(core * 8 + k, sel)
            sent_grid[k, sel] = send(("grid", k, sel), place, place, sibling)

    def quad(q):
        for k in (2 * q, 2 * q + 1):
            for sel in range(2):
                arrived(("grid", k, sel), place_of((1 - core) * 8 + k, sel), sibling)
                sent_grid[k, sel].wait_send()
                sent[:] = [copy for copy in sent if copy is not sent_grid[k, sel]]

        def body(i, carry):
            rows_of = [
                [pl.ds(pl.multiple_of(g * 1024 + i * 64 + r, 16), 16) for g in (2 * q, 2 * q + 1, 8 + 2 * q, 9 + 2 * q)]
                for r in range(0, 64, 16)]
            values = [butterfly([grid[place, :] for place in places]) for places in rows_of]
            for places, results in zip(rows_of, values):
                for place, result in zip(places, results):
                    grid[place, :] = result
            return carry

        lax.fori_loop(0, 16, body, 0)

    def take_ct(step):
        if step == 0:
            arrived("ct", ct_land.at[core], near)
            send("ct2", ct_land.at[core], ct_land.at[core], sibling)
            ct_other[own_rows, :] = ct_land[core].astype(BF16)
        else:
            arrived("ct2", ct_land.at[1 - core], sibling)
            ct_other[mate_rows, :] = ct_land[1 - core].astype(BF16)

    def hop_x(k, d):
        if d == 0:
            arrived(("feed", k), xs(k, x), route[k])
            send(("xr", k), xs(k, x), xs(k, x), right_x)
            send(("xl", k), xs(k, x), xs(k, x), left_x)
        elif d == 1:
            arrived(("xr", k), xs(k, x - 1), left_x)
            if k % 2 == 0:
                send(("xe", k), xs(k, x - 1), xs(k, x - 1), right_x)
            arrived(("xl", k), xs(k, x + 1), right_x)
            if k % 2 == 1:
                send(("xe", k), xs(k, x + 1), xs(k, x + 1), left_x)
        else:
            arrived(("xe", k), xs(k, x + 2), left_x if k % 2 == 0 else right_x)

    def hop_z(k, d):
        if d == 0:
            arrived(("feed", k), zs(k, z), route[k])
            send(("zr", k, 1), zs(k, z), zs(k, z), right_z)
            send(("zl", k, 1), zs(k, z), zs(k, z), left_z)
        elif d < 4:
            arrived(("zr", k, d), zs(k, z - d), left_z)
            if d < 3 or k % 2 == 0:
                send(("zr", k, d + 1), zs(k, z - d), zs(k, z - d), right_z)
            arrived(("zl", k, d), zs(k, z + d), right_z)
            if d < 3 or k % 2 == 1:
                send(("zl", k, d + 1), zs(k, z + d), zs(k, z + d), left_z)
        else:
            if k % 2 == 0:
                arrived(("zr", k, 4), zs(k, z - 4), left_z)
            else:
                arrived(("zl", k, 4), zs(k, z + 4), right_z)

    def hop_y(k):
        arrived(("feed", k, "n"), xo.at[k, pl.ds(0, 256)], near)
        arrived(("feed", k, "f"), xo.at[k, pl.ds(256, 256)], far)

    for step in " ".join(ORDER).split():
        kind, k, d = step[0], int(step[1]), int(step[2])
        if kind == "x":
            hop_x(k, d)
        elif kind == "z":
            hop_z(k, d)
        elif kind == "y":
            hop_y(k)
        elif kind == "c":
            take_ct(k)
        elif kind == "p":
            prepare(k)
        elif kind == "m":
            process(k)
        else:
            quad(k)

    def last(i, carry):
        at = (i // 32) * 8192 + (i // 16 % 2) * 1024 + (i % 16) * 64
        rows_of = [
            [pl.ds(pl.multiple_of(at + q * 2048 + r, 16), 16) for q in range(4)] for r in range(0, 64, 16)]
        values = [butterfly([grid[place, :] for place in places]) for places in rows_of]
        for places, results in zip(rows_of, values):
            for place, result in zip(places, results):
                grid[place, :] = result
        return carry

    lax.fori_loop(0, 64, last, 0)
    to_scalar.wait()
    code = tok | (x << 2) | (z << 4)
    lanes = lax.broadcasted_iota(jnp.int32, (128, 128), 0)

    def place_in(n):
        return wrap(me + 1 + n // 8, 8), n % 8

    def gather(n, to):
        piece, b = place_in(n)
        for r in range(0, 128, 8):
            to[r:r + 8, :] = jnp.concatenate(
                [grid[pl.ds(index_s[piece * 8 + b, r + k], 1), :] for k in range(8)], axis=0)

    def pick(n, got):
        piece, b = place_in(n)
        m = samples[pl.ds(core * 64 + piece * 8 + b, 1), :]
        picked = jnp.where(lanes == ((m >> 8) & 127), got[...].T, 0.0)
        value = jnp.sum(picked, axis=0, keepdims=True)
        odd = (m >> 20) & code
        odd = odd ^ (odd >> 4)
        odd = odd ^ (odd >> 2)
        odd = odd ^ (odd >> 1)
        mine[piece, pl.ds(b, 1), :] = jnp.where((odd & 1) == 1, -value, value)

    def xt_copy(d, piece, member):
        return pltpu.make_async_remote_copy(
            src_ref=mine.at[piece], dst_ref=land_xt.at[d - 1], send_sem=send_small.at[d - 1],
            recv_sem=recv_small.at[d - 1], device_id=xt_device(member), device_id_type=MESH)

    def gather_step(i, carry):
        gather(2 * i + 1, rows_b)
        pick(2 * i, rows)
        gather(jnp.minimum(2 * i + 2, 63), rows)
        pick(2 * i + 1, rows_b)

        @pl.when(jnp.logical_and(i % 4 == 3, i < 28))
        def _():
            d = i // 4 + 1
            piece = wrap(me + d, 8)
            xt_copy(d, piece, piece).start()

        return carry

    gather(0, rows)
    lax.fori_loop(0, 32, gather_step, 0)
    total = mine[me]
    for d in range(1, 8):
        xt_copy(d, wrap(me + d, 8), wrap(me - d, 8)).wait_recv()
        total = total + land_xt[d - 1]
    red[...] = total

    def column_copy(source, target):
        return pltpu.make_async_remote_copy(
            src_ref=red, dst_ref=land_z.at[source], send_sem=send_small.at[7 + target],
            recv_sem=recv_small.at[7 + source], device_id=column_device(target // 2, target % 2), device_id_type=MESH)

    here = z * 2 + core
    for dz, dc in column:
        copy = column_copy(here, wrap(z + dz, 8) * 2 + (core ^ dc))
        copy.start()
        sent.append(copy)
    land_z[here] = total
    for dz, dc in column:
        column_copy(wrap(z - dz, 8) * 2 + (core ^ dc), here).wait_recv()
    scale = float(1024 * 134217728) ** (-0.5)

    for c in range(2):
        total = land_z[c]
        for i in range(1, 8):
            total = total + land_z[2 * i + c]
        full[me, probe, c] = total * scale

    def plane_copy(n, row, row_probe, member, other_probe):
        place = full.at[row, row_probe]
        return pltpu.make_async_remote_copy(
            src_ref=place, dst_ref=place, send_sem=send_small.at[23 + n], recv_sem=recv_small.at[23 + n],
            device_id=plane_device(member, other_probe), device_id_type=MESH)

    for n, (d, dp) in enumerate(plane):
        copy = plane_copy(n, me, probe, wrap(me + d, 8), probe ^ dp)
        copy.start()
        sent.append(copy)
    for n, (d, dp) in enumerate(plane):
        source = wrap(me - d, 8)
        plane_copy(n, source, probe ^ dp, source, probe ^ dp).wait_recv()

    count = 16384.0

    def mean(value):
        value = jnp.sum(value, axis=(0, 1))
        return jnp.sum(jnp.sum(value, axis=0, keepdims=True), axis=1, keepdims=True) / count

    first, second = full[:, 0], full[:, 1]
    unit = first * lax.rsqrt(mean(first * first) + 1e-06)
    rest = second - mean(unit * second) * unit
    last = rest * lax.rsqrt(mean(rest * rest) + 1e-06)
    by_probe = probe == 0
    for i in range(8):
        at = slice(i * 8, (i + 1) * 8)
        sketch_ref[0, at, :] = jnp.where(by_probe, first[i, 0], first[i, 1])
        sketch_ref[1, at, :] = jnp.where(by_probe, second[i, 0], second[i, 1])
        basis_ref[0, at, :] = jnp.where(by_probe, unit[i, 0], unit[i, 1])
        basis_ref[1, at, :] = jnp.where(by_probe, last[i, 0], last[i, 1])
    for d in range(1, 8):
        xt_copy(d, wrap(me + d, 8), wrap(me + d, 8)).wait_send()
    for copy in sent:
        copy.wait_send()


def whole(tokens_x, cot_t, signs, samples):
    shape = jax.ShapeDtypeStruct((2, 64, 128), F32)
    return pl.pallas_call(
        whole_kernel,
        out_shape=(shape, shape),
        in_specs=[pl.BlockSpec(memory_space=pltpu.HBM)] * 4,
        out_specs=(pl.BlockSpec(memory_space=pltpu.VMEM), pl.BlockSpec(memory_space=pltpu.VMEM)),
        scratch_shapes=[
            pltpu.VMEM((512, 2048), BF16),
            pltpu.VMEM((128, 1024), BF16),
            pltpu.VMEM((64, 768), BF16),
            pltpu.VMEM((512, SIDE), BF16),
            pltpu.VMEM((4, 128, SIDE), F32),
            pltpu.VMEM((3, 64, SIDE), F32),
            pltpu.VMEM((512, SIDE), F32),
            pltpu.VMEM((2, 4096, 128), jnp.int32),
            pltpu.VMEM((224, 512), BF16),
            pltpu.VMEM((224, 512), F32),
            pltpu.VMEM((224, 512), F32),
            pltpu.VMEM((2, 224, 512), F32),
            pltpu.VMEM((512, 512), BF16),
            pltpu.VMEM((512, 512), BF16),
            pltpu.VMEM((SIDE, SIDE), BF16),
            pltpu.VMEM((8, 512, SIDE), F32),
            pltpu.VMEM((8, 512, SIDE), F32),
            pltpu.VMEM((8, 512, SIDE), F32),
            pltpu.VMEM((16384, 128), F32),
            pltpu.VMEM((128, 128), jnp.int32),
            pltpu.VMEM((64, 128), jnp.int32),
            pltpu.SMEM((64, 128), jnp.int32),
            pltpu.VMEM((128, 128), F32),
            pltpu.VMEM((128, 128), F32),
            pltpu.VMEM((8, 8, 128), F32),
            pltpu.VMEM((7, 8, 128), F32),
            pltpu.VMEM((8, 128), F32),
            pltpu.VMEM((16, 8, 128), F32),
            pltpu.VMEM((8, 2, 2, 8, 128), F32),
            pltpu.SemaphoreType.DMA((8,)),
            pltpu.SemaphoreType.DMA((88,)),
            pltpu.SemaphoreType.DMA((88,)),
            pltpu.SemaphoreType.DMA((38,)),
            pltpu.SemaphoreType.DMA((38,)),
        ],
        compiler_params=pltpu.CompilerParams(
            collective_id=0, has_side_effects=True, vmem_limit_bytes=56 << 20),
        cost_estimate=pl.CostEstimate(flops=8 << 30, bytes_accessed=24 << 20, transcendentals=0),
        name="whole",
    )(tokens_x, cot_t, signs, samples)


def on_device(tokens_x, cotangent, signs, samples):
    sketch, basis = whole(tokens_x, cotangent[0].T, signs.reshape(8192, 128), samples.reshape(128, 128))
    return sketch.reshape(2, 8192), basis.reshape(2, 8192)


def solution(mesh):
    in_specs = (P("tok", None), P("probe", "tok", "param"), P(("param", "tok")), P())
    out_specs = (P(None, "probe"), P(None, "probe"))
    return jax.shard_map(
        on_device, mesh=mesh, in_specs=in_specs, out_specs=out_specs, check_vma=False
    )
```

time: 78.8 us -> 71.4 us (0.906)
  Pallas kernels: 75.1 us -> 69 us
  local copies, waits for them, and re-layouts: 2.95 us -> 1.63 us
    pallas_call x1, Pallas kernels: 75.1 us -> 69 us  [whole(): pl.pallas_call(whole_kernel, out_shape=(shape, shape), in_specs=[pl.Block...]
    unnamed x2 -> x0, local copies, waits for them, and re-layouts: 2.95 us -> none
    reshape x0 -> x1, local copies, waits for them, and re-layouts: none -> 1.63 us  [on_device(): return (sketch.reshape(2, 8192), basis.reshape(2, 8192))]
where the time goes in v3:
time: 71.4 us; the launch traced here: 71.3 us
  Pallas kernels  69 us (97%)
  local copies, waits for them, and re-layouts  1.63 us (2%)
    pallas_call x1, Pallas kernels, whole(): pl.pallas_call(whole_kernel, out_shape=(shape, shape), in_specs=[pl.Block...  69 us
    reshape x1, local copies, waits for them, and re-layouts, on_device(): return (sketch.reshape(2, 8192), basis.reshape(2, 8192))  1.63 us

profile of v3, /device:TPU:1, one launch (start us, length us, event | category | flops | bytes accessed | tf_op | source)
XLA Modules:
  0.0 71.3 jit_solution(403112889604530082)
XLA Ops:
  0.6 69.0 %whole.1 = (f32[2,64,128]{2,1,0:T(8,128)}, f32[2,64,128]{2,1,0:T(8,128)}) custom-call(bf16[512,8192]{1,0:T(8,128)(2,1)} %x_ref.1, bf16[224,512]{1,0:T(8,128)(2,1)} %bitcast.14, s32[8192,128]{1,0:T(8,128)} %bitcast.13, s32[128,128]{1,0:T(8,128)} %bitcast.15), custom_call_target="tpu_custom_call" | custom-call | flops 8589934592 | bytes 25165824 | tf_op jit(solution)/shard_map/whole/pallas_call | solution.py:434
  69.7 1.6 %copy_bitcast_fusion = (f32[2,8192]{1,0:T(2,128)}, f32[2,8192]{1,0:T(2,128)}) fusion(f32[1,2,64,128]{3,2,1,0:T(8,128)} %bitcast.12, f32[1,2,64,128]{3,2,1,0:T(8,128)} %bitcast.11), kind=kLoop, calls=%fused_computation | loop fusion | bytes 262144 | tf_op jit(solution)/shard_map/reshape | solution.py:484

commit v4 on v3

--- a/solution.py
+++ b/solution.py
@@ -89,8 +89,8 @@
     def plane_device(member, other_probe):
         return device(z, member // 2, core, member % 2, other_probe)
 
-    column = [(dz, dc) for dz in range(8) for dc in range(2)][1:]
-    plane = [(d, dp) for d in range(8) for dp in range(2)][1:]
+    column = [(dz, dc) for dz in (4, 3, 5, 2, 6, 1, 7, 0) for dc in (1, 0)][:-1]
+    plane = [(d, dp) for d in (4, 5, 3, 2, 6, 7, 1, 0) for dp in (1, 0)][:-1]
 
     mine_at = pl.multiple_of(tok * half + core * 2048, 128)
     theirs = pl.multiple_of((1 - tok) * half + core * 2048, 128)
@@ -139,6 +139,9 @@
     def xs(k, i):
         return xo.at[k, pl.ds(pl.multiple_of(128 * wrap(i, RING_X), 128), 128)]
 
+    def xs_part(k, i, part):
+        return xo.at[k, pl.ds(pl.multiple_of(128 * wrap(i, RING_X) + part, 64), 64)]
+
     def zs(k, i):
         return xo.at[k, pl.ds(pl.multiple_of(64 * wrap(i, RING_Z), 64), 64)]
 
@@ -151,6 +154,7 @@
     pl.semaphore_wait(barrier, len(partners))
 
     route = {}
+    split = {k for _, k in FEED if k != 7 and sum(entry[1] == k for entry in FEED) == 2}
     for side, k in FEED:
         target = near if side == "n" else far
         if k == "ct":
@@ -165,7 +169,10 @@
             send(("feed", 7, side), yf.at[part], xo.at[7, part], target)
         else:
             route[k] = target
-            if k < 4:
+            if k in split:
+                part = 0 if side == "n" else 64
+                send(("feed", k, side), xf.at[k, pl.ds(part, 64)], xs_part(k, x, part), target)
+            elif k < 4:
                 send(("feed", k), xf.at[k], xs(k, x), target)
             else:
                 send(("feed", k), zf.at[k - 4], zs(k, z), target)
@@ -244,7 +251,7 @@
                     grid[place, :] = result
             return carry
 
-        lax.fori_loop(0, 16, body, 0)
+        lax.fori_loop(0, 16, body, 0, unroll=4)
 
     def take_ct(step):
         if step == 0:
@@ -257,7 +264,11 @@
 
     def hop_x(k, d):
         if d == 0:
-            arrived(("feed", k), xs(k, x), route[k])
+            if k in split:
+                arrived(("feed", k, "n"), xs_part(k, x, 0), near)
+                arrived(("feed", k, "f"), xs_part(k, x, 64), far)
+            else:
+                arrived(("feed", k), xs(k, x), route[k])
             send(("xr", k), xs(k, x), xs(k, x), right_x)
             send(("xl", k), xs(k, x), xs(k, x), left_x)
         elif d == 1:
@@ -319,7 +330,7 @@
                 grid[place, :] = result
         return carry
 
-    lax.fori_loop(0, 64, last, 0)
+    lax.fori_loop(0, 64, last, 0, unroll=4)
     to_scalar.wait()
     code = tok | (x << 2) | (z << 4)
     lanes = lax.broadcasted_iota(jnp.int32, (128, 128), 0)
@@ -473,7 +484,7 @@
             pltpu.SemaphoreType.DMA((38,)),
         ],
         compiler_params=pltpu.CompilerParams(
-            collective_id=0, has_side_effects=True, vmem_limit_bytes=56 << 20),
+            collective_id=0, has_side_effects=True, vmem_limit_bytes=55104 << 10),
         cost_estimate=pl.CostEstimate(flops=8 << 30, bytes_accessed=24 << 20, transcendentals=0),
         name="whole",
     )(tokens_x, cot_t, signs, samples)

time: 71.4 us -> 68.3 us (0.957)
  Pallas kernels: 69 us -> 66.8 us
  local copies, waits for them, and re-layouts: 1.63 us -> 0.75 us
    pallas_call x1, Pallas kernels: 69 us -> 66.8 us  [whole(): pl.pallas_call(whole_kernel, out_shape=(shape, shape), in_specs=[pl.Block...]
    reshape x1, local copies, waits for them, and re-layouts: 1.63 us -> 0.75 us  [on_device(): return (sketch.reshape(2, 8192), basis.reshape(2, 8192))]
where the time goes in v4:
time: 68.3 us; the launch traced here: 68.2 us
  Pallas kernels  66.8 us (98%)
  local copies, waits for them, and re-layouts  0.75 us (1%)
    pallas_call x1, Pallas kernels, whole(): pl.pallas_call(whole_kernel, out_shape=(shape, shape), in_specs=[pl.Block...  66.8 us

profile of v4, /device:TPU:1, one launch (start us, length us, event | category | flops | bytes accessed | tf_op | source)
XLA Modules:
  0.0 68.2 jit_solution(8743820748361069628)
XLA Ops:
  0.6 66.8 %whole.1 = (f32[2,64,128]{2,1,0:T(8,128)S(1)}, f32[2,64,128]{2,1,0:T(8,128)S(1)}) custom-call(bf16[512,8192]{1,0:T(8,128)(2,1)} %x_ref.1, bf16[224,512]{1,0:T(8,128)(2,1)} %bitcast.14, s32[8192,128]{1,0:T(8,128)} %bitcast.13, s32[128,128]{1,0:T(8,128)} %bitcast.15), custom_call_target="tpu_custom_call" | custom-call | flops 8589934592 | bytes 25165824 | tf_op jit(solution)/shard_map/whole/pallas_call | solution.py:445
  67.4 0.8 %copy_bitcast_fusion = (f32[2,8192]{1,0:T(2,128)}, f32[2,8192]{1,0:T(2,128)}) fusion(f32[1,2,64,128]{3,2,1,0:T(8,128)S(1)} %bitcast.12, f32[1,2,64,128]{3,2,1,0:T(8,128)S(1)} %bitcast.11), kind=kLoop, calls=%fused_computation | loop fusion | bytes 262144 | tf_op jit(solution)/shard_map/reshape | solution.py:495

commit v5 on v4

--- a/solution.py
+++ b/solution.py
@@ -106,7 +106,7 @@
         pltpu.make_async_copy(
             signs_ref.at[pl.ds(pl.multiple_of(core * half, half), half)], sg.at[core], local_sem.at[6]),
     ]
-    for load in loads:
+    for load in loads[:2]:
         load.start()
 
     barrier = pltpu.get_barrier_semaphore()
@@ -114,6 +114,8 @@
     partners += [column_device(wrap(z + dz, 8), core ^ dc) for dz, dc in column]
     for partner in partners:
         pl.semaphore_signal(barrier, inc=1, device_id=partner, device_id_type=MESH)
+    for load in loads[2:]:
+        load.start()
 
     numbers = {}
     sent = []

time: 68.3 us -> 68.3 us (level)
  no operation moved by 1% of the time
where the time goes in v5:
time: 68.3 us; the launch traced here: 68.2 us
  Pallas kernels  66.8 us (98%)
  local copies, waits for them, and re-layouts  0.75 us (1%)
    pallas_call x1, Pallas kernels, whole(): pl.pallas_call(whole_kernel, out_shape=(shape, shape), in_specs=[pl.Block...  66.8 us

profile of v5, /device:TPU:1, one launch (start us, length us, event | category | flops | bytes accessed | tf_op | source)
XLA Modules:
  0.0 68.2 jit_solution(8801747080867667638)
XLA Ops:
  0.6 66.8 %whole.1 = (f32[2,64,128]{2,1,0:T(8,128)S(1)}, f32[2,64,128]{2,1,0:T(8,128)S(1)}) custom-call(bf16[512,8192]{1,0:T(8,128)(2,1)} %x_ref.1, bf16[224,512]{1,0:T(8,128)(2,1)} %bitcast.14, s32[8192,128]{1,0:T(8,128)} %bitcast.13, s32[128,128]{1,0:T(8,128)} %bitcast.15), custom_call_target="tpu_custom_call" | custom-call | flops 8589934592 | bytes 25165824 | tf_op jit(solution)/shard_map/whole/pallas_call | solution.py:447
  67.4 0.8 %copy_bitcast_fusion = (f32[2,8192]{1,0:T(2,128)}, f32[2,8192]{1,0:T(2,128)}) fusion(f32[1,2,64,128]{3,2,1,0:T(8,128)S(1)} %bitcast.12, f32[1,2,64,128]{3,2,1,0:T(8,128)S(1)} %bitcast.11), kind=kLoop, calls=%fused_computation | loop fusion | bytes 262144 | tf_op jit(solution)/shard_map/reshape | solution.py:497
